TPU v7x, 32 devices: a whole 2x2x4 slice. The times are simulated.
32 devices in a mesh: leaf: 8 (over z, x), sep: 4 (over y, core).
Axes of the slice: x: 2, y: 2, z: 4, core: 2. Of those that a mesh axis runs over, the one named last changes fastest.
Arguments:
- right_side: float32 [32768, 128], P(('leaf', 'sep')), may hold values from -6 to 6
- inverse_root: bfloat16 [8192, 8192], P(('leaf', 'sep')), may hold values from -1 to 3
- inverse_middle: bfloat16 [8192, 4096], P(('leaf', 'sep')), may hold values from -1 to 3
- inverse_lower: bfloat16 [16384, 4096], P(('leaf', 'sep')), may hold values from -1 to 3
- update_middle: bfloat16 [8192, 128], P(('leaf', 'sep')), may hold values from -0.09375 to 0.09375
- update_lower: bfloat16 [16384, 64], P(('leaf', 'sep')), may hold values from -0.09375 to 0.09375
- target_middle: int32 [32, 1], P(('leaf', 'sep')), may hold values from 0 to 31
- target_lower: int32 [32, 1], P(('leaf', 'sep')), may hold values from 0 to 63
Outputs:
- solution: float32 [32768, 128], P(('leaf', 'sep'))
All inputs are finite; a program needn't handle non-finite values.
Results may differ from a plain program's by a relative error of at most 0.0037.
Values may be sent and summed in bfloat16 or wider, within the bound.
A program may use at most 64 MiB of HBM per device.

v0:
```python
import jax
import jax.numpy as jnp
from jax import lax
from jax.sharding import PartitionSpec as P

BLOCK = 8


def from_partner(block, axis, distance):
    count = lax.axis_size(axis)
    route = []
    for low in range(count):
        high = low | 1 << distance
        if high != low and high < count:
            route += [(low, high), (high, low)]
    return lax.ppermute(block, axis, route)


def on_device(
    right_side,
    inverse_root,
    inverse_middle,
    inverse_lower,
    update_middle,
    update_lower,
    target_middle,
    target_lower,
):
    leaf_index = lax.axis_index("leaf")
    leaf_count = lax.axis_size("leaf")
    leaf_bits = leaf_count.bit_length() - 1
    dev_rows = inverse_root.shape[0]
    width = right_side.shape[1]
    root_side = right_side[:dev_rows]
    middle_side = right_side[dev_rows : 2 * dev_rows]
    lower_side = right_side[2 * dev_rows :]

    def collect(piece, depth_bits):
        panel = lax.all_gather(piece, "sep", axis=0, tiled=True)
        for bit_index in range(depth_bits):
            partner = from_partner(panel, "leaf", bit_index)
            upper = leaf_index >> bit_index & 1 == 1
            first = jnp.where(upper, partner, panel)
            second = jnp.where(upper, panel, partner)
            panel = jnp.concatenate([first, second], axis=0)
        return panel

    def apply_inverse(inverse, words, depth_bits):
        panel = collect(words, depth_bits)
        return jnp.dot(inverse, panel, preferred_element_type=jnp.float32)

    def halve_whole(current, depth_bits):
        for bit_index in reversed(range(depth_bits)):
            half = current.shape[0] // 2
            upper = leaf_index >> bit_index & 1 == 1
            keep = jnp.where(upper, current[half:], current[:half])
            give = jnp.where(upper, current[:half], current[half:])
            current = keep + from_partner(give, "leaf", bit_index)
        return current

    def reduce_slots(partial_value, depth_bits):
        current = halve_whole(partial_value, depth_bits)
        return lax.psum_scatter(current, "sep", scatter_dimension=0, tiled=True)

    def selector(targets, blocks):
        return (jnp.arange(blocks, dtype=jnp.int32)[:, None] == targets[0][None, :]).astype(
            jnp.float32
        )

    def place_slots(summed, targets, blocks):
        onehot = selector(targets, blocks)
        flat = summed.reshape(targets.shape[1], BLOCK * width)
        placed = jnp.dot(onehot, flat, precision=lax.Precision.HIGHEST)
        return placed.reshape(blocks * BLOCK, width)

    def pick_slots(table, targets, blocks):
        onehot = selector(targets, blocks)
        flat = table.astype(jnp.float32).reshape(blocks, BLOCK * width)
        picked = jnp.dot(onehot.T, flat, precision=lax.Precision.HIGHEST)
        return picked.reshape(targets.shape[1] * BLOCK, width).astype(jnp.bfloat16)

    contract_rows = (((0,), (0,)), ((), ()))
    lower_blocks = 2 * dev_rows // BLOCK
    middle_blocks = dev_rows // BLOCK
    lower_words = lower_side.astype(jnp.bfloat16)
    lower_values = apply_inverse(inverse_lower, lower_words, leaf_bits - 2)
    lower_partial = lax.dot_general(
        update_lower, lower_words, contract_rows, preferred_element_type=jnp.float32
    )
    lower_accum = place_slots(
        reduce_slots(lower_partial, leaf_bits - 2), target_lower, lower_blocks
    )
    middle_words = (middle_side - lower_accum[dev_rows:]).astype(jnp.bfloat16)
    middle_values = apply_inverse(inverse_middle, middle_words, leaf_bits - 1)
    middle_partial = lax.dot_general(
        update_middle, middle_words, contract_rows, preferred_element_type=jnp.float32
    )
    middle_accum = place_slots(
        reduce_slots(middle_partial, leaf_bits - 1), target_middle, middle_blocks
    )
    root_words = (root_side - (lower_accum[:dev_rows] + middle_accum)).astype(jnp.bfloat16)
    root_solution = apply_inverse(inverse_root, root_words, leaf_bits)
    root_rounded = root_solution.astype(jnp.bfloat16)
    middle_slots = collect(pick_slots(root_rounded, target_middle, middle_blocks), leaf_bits - 1)
    middle_solution = middle_values - jnp.dot(
        update_middle, middle_slots, preferred_element_type=jnp.float32
    )
    middle_rounded = middle_solution.astype(jnp.bfloat16)
    table = jnp.concatenate([root_rounded, middle_rounded], axis=0)
    lower_slots = collect(pick_slots(table, target_lower, lower_blocks), leaf_bits - 2)
    lower_solution = lower_values - jnp.dot(
        update_lower, lower_slots, preferred_element_type=jnp.float32
    )
    return jnp.concatenate([root_solution, middle_solution, lower_solution], axis=0)


def solution(mesh):
    in_specs = (
        P(("leaf", "sep"), None),
        P(("leaf", "sep"), None),
        P(("leaf", "sep"), None),
        P(("leaf", "sep"), None),
        P(("leaf", "sep"), None),
        P(("leaf", "sep"), None),
        P(("leaf", "sep"), None),
        P(("leaf", "sep"), None),
    )
    out_specs = P(("leaf", "sep"), None)
    return jax.shard_map(
        on_device, mesh=mesh, in_specs=in_specs, out_specs=out_specs, check_vma=False
    )
```

profile of v0, /device:TPU:0, one launch (start us, length us, event | category | flops | bytes accessed | tf_op | source)
XLA Modules:
  0.0 152.9 jit_solution(7578756123601498769)
XLA Ops:
  0.0 0.0 copy-start
  0.0 1.3 fusion.44
  1.3 3.0 %collective-permute-start = (f32[32,128]{1,0:T(8,128)S(1)}, f32[32,128]{1,0:T(8,128)S(1)}, u32[]{:S(2)}, u32[]{:S(2)}) collective-permute-start(f32[32,128]{1,0:T(8,128)S(1)} %slice_select_fusion.2), channel_id=1, source_target_pairs={{0,4},{4,0},{8,12},{12,8},{16,20},{20,16},{24,28},{28,24},{1,5},{5... | collective-permute-start | bytes 49160 | tf_op jit(solution)/shard_map/ppermute | solution.py:16
  5.0 1.2 dynamic-slice
  6.9 0.0 collective-permute-done
  6.9 10.7 %all-reduce = f32[32,128]{1,0:T(8,128)S(1)} all-reduce(f32[32,128]{1,0:T(8,128)S(1)} %select_add_fusion.2), channel_id=2, replica_groups=mesh['leaf'=8,'sep'=4] {'sep'}, use_global_device_ids=true, to_apply=%region_0.1.clone | all-reduce | flops 4096 | bytes 32768
  17.6 0.1 broadcast_multiply_fusion
  17.7 0.9 subtract_convert_fusion.1
  18.6 1.1 convolution_bitcast_fusion
  19.7 1.6 %collective-permute-start.1 = (f32[64,128]{1,0:T(8,128)S(1)}, f32[64,128]{1,0:T(8,128)S(1)}, u32[]{:S(2)}, u32[]{:S(2)}) collective-permute-start(f32[64,128]{1,0:T(8,128)S(1)} %slice_select_fusion), channel_id=1, source_target_pairs={{0,8},{8,0},{4,12},{12,4},{16,24},{24,16},{20,28},{28,20},{1,9},{9... | collective-permute-start | bytes 98312 | tf_op jit(solution)/shard_map/ppermute | solution.py:16
  22.0 1.7 %collective-permute-done.1 = f32[64,128]{1,0:T(8,128)S(1)} collective-permute-done((f32[64,128]{1,0:T(8,128)S(1)}, f32[64,128]{1,0:T(8,128)S(1)}, u32[]{:S(2)}, u32[]{:S(2)}) %collective-permute-start.1) | collective-permute-done | bytes 32800 | tf_op jit(solution)/shard_map/ppermute | solution.py:16
  23.7 0.7 collective-permute-start.2
  24.4 3.1 %collective-permute-done.2 = f32[32,128]{1,0:T(8,128)S(1)} collective-permute-done((f32[32,128]{1,0:T(8,128)S(1)}, f32[32,128]{1,0:T(8,128)S(1)}, u32[]{:S(2)}, u32[]{:S(2)}) %collective-permute-start.2) | collective-permute-done | bytes 16416 | tf_op jit(solution)/shard_map/ppermute | solution.py:16
  27.5 10.1 %all-reduce.1 = f32[32,128]{1,0:T(8,128)S(1)} all-reduce(f32[32,128]{1,0:T(8,128)S(1)} %select_add_fusion.1), channel_id=3, replica_groups=mesh['leaf'=8,'sep'=4] {'sep'}, use_global_device_ids=true, to_apply=%region_1.2.clone | all-reduce | flops 4096 | bytes 32768
  37.6 0.1 slice_add_fusion
  37.7 0.9 subtract_convert_fusion
  38.7 5.8 %all_gather.15 = bf16[1024,128]{1,0:T(8,128)(2,1)S(1)} all-gather(bf16[256,128]{1,0:T(8,128)(2,1)S(1)} %subtract_convert_fusion), channel_id=1, replica_groups=mesh['leaf'=8,'sep'=4] {'sep'}, dimensions={0}, use_global_device_ids=true | all-gather | bytes 327680 | tf_op jit(solution)/shard_map/all_gather | solution.py:39
  44.5 0.7 collective-permute-start.3
  45.1 7.9 %collective-permute-done.3 = bf16[1024,128]{1,0:T(8,128)(2,1)S(1)} collective-permute-done((bf16[1024,128]{1,0:T(8,128)(2,1)S(1)}, bf16[1024,128]{1,0:T(8,128)(2,1)S(1)}, u32[]{:S(2)}, u32[]{:S(2)}) %collective-permute-start.3) | collective-permute-done | bytes 262176 | tf_op jit(solution)/shard_map/ppermute | solution.py:16
  53.0 0.1 broadcast_select_fusion.11
  53.1 1.6 %collective-permute-start.4 = (bf16[2048,128]{1,0:T(8,128)(2,1)S(1)}, bf16[2048,128]{1,0:T(8,128)(2,1)S(1)}, u32[]{:S(2)}, u32[]{:S(2)}) collective-permute-start(bf16[2048,128]{1,0:T(8,128)(2,1)S(1)} %pad_maximum_fusion.1), channel_id=1, source_target_pairs={{0,8},{8,0},{4,12},{12,4},{16,24},{24,16},{20,28},{28,20},{1,9},{9... | collective-permute-start | bytes 1572872 | tf_op jit(solution)/shard_map/ppermute | solution.py:16
  54.8 11.8 %collective-permute-done.4 = bf16[2048,128]{1,0:T(8,128)(2,1)S(1)} collective-permute-done((bf16[2048,128]{1,0:T(8,128)(2,1)S(1)}, bf16[2048,128]{1,0:T(8,128)(2,1)S(1)}, u32[]{:S(2)}, u32[]{:S(2)}) %collective-permute-start.4) | collective-permute-done | bytes 524320 | tf_op jit(solution)/shard_map/ppermute | solution.py:16
  66.6 0.2 broadcast_select_fusion.7
  66.8 1.1 pad_maximum_fusion
  67.8 2.6 %collective-permute-start.5 = (bf16[4096,128]{1,0:T(8,128)(2,1)}, bf16[4096,128]{1,0:T(8,128)(2,1)}, u32[]{:S(2)}, u32[]{:S(2)}) collective-permute-start(bf16[4096,128]{1,0:T(8,128)(2,1)} %pad_maximum_fusion), channel_id=1, source_target_pairs={{0,16},{16,0},{4,20},{20,4},{8,24},{24,8},{12,28},{28,12},{1,17},{... | collective-permute-start | bytes 3145736 | tf_op jit(solution)/shard_map/ppermute | solution.py:16
  70.4 5.8 %all_gather.16 = bf16[1024,128]{1,0:T(8,128)(2,1)S(1)} all-gather(bf16[256,128]{1,0:T(8,128)(2,1)S(1)} %subtract_convert_fusion.1), channel_id=1, replica_groups=mesh['leaf'=8,'sep'=4] {'sep'}, dimensions={0}, use_global_device_ids=true | all-gather | bytes 327680 | tf_op jit(solution)/shard_map/all_gather | solution.py:39
  76.2 0.7 collective-permute-start.6
  76.9 1.0 slice.81
  77.8 0.0 copy-done.3
  77.9 7.0 %collective-permute-done.6 = bf16[1024,128]{1,0:T(8,128)(2,1)} collective-permute-done((bf16[1024,128]{1,0:T(8,128)(2,1)S(1)}, bf16[1024,128]{1,0:T(8,128)(2,1)}, u32[]{:S(2)}, u32[]{:S(2)}) %collective-permute-start.6) | collective-permute-done | bytes 262176 | tf_op jit(solution)/shard_map/ppermute | solution.py:16
  84.9 1.1 broadcast_select_fusion.9
  85.9 0.0 copy-start.1
  85.9 0.7 copy-done.1
  86.7 0.8 pad_maximum_fusion.2
  87.5 1.6 %collective-permute-start.7 = (bf16[2048,128]{1,0:T(8,128)(2,1)}, bf16[2048,128]{1,0:T(8,128)(2,1)}, u32[]{:S(2)}, u32[]{:S(2)}) collective-permute-start(bf16[2048,128]{1,0:T(8,128)(2,1)} %pad_maximum_fusion.2), channel_id=1, source_target_pairs={{0,8},{8,0},{4,12},{12,4},{16,24},{24,16},{20,28},{28,20},{1,9},{9... | collective-permute-start | bytes 1572872 | tf_op jit(solution)/shard_map/ppermute | solution.py:16
  89.1 26.3 %collective-permute-done.5 = bf16[4096,128]{1,0:T(8,128)(2,1)} collective-permute-done((bf16[4096,128]{1,0:T(8,128)(2,1)}, bf16[4096,128]{1,0:T(8,128)(2,1)}, u32[]{:S(2)}, u32[]{:S(2)}) %collective-permute-start.5) | collective-permute-done | bytes 1048608 | tf_op jit(solution)/shard_map/ppermute | solution.py:16
  115.3 1.6 %broadcast_select_fusion.1 = (bf16[4096,128]{1,0:T(8,128)(2,1)S(1)}, bf16[4096,128]{1,0:T(8,128)(2,1)S(1)}) fusion(bf16[4096,128]{1,0:T(8,128)(2,1)} %collective-permute-done.5, pred[]{:T(512)S(6)} %eq.94, bf16[2048,128]{1,0:T(8,128)(2,1)S(1)} %get-tuple-element.12, bf16[2048,128]{1,0:T(8,128)(2,1)S(1)} %get-tuple-element.11), kind=kLoop, calls=%fused_computation.18 | loop fusion | flops 3145728 | bytes 4194305 | tf_op jit(solution)/shard_map/jit(_where)/select_n | solution.py:43
  117.0 2.2 %fusion.42 = (bf16[256,128]{0,1:T(8,128)(2,1)S(1)}, f32[256,128]{0,1:T(8,128)}) fusion(bf16[256,8192]{1,0:T(8,128)(2,1)S(1)} %copy-done.7, bf16[4096,128]{1,0:T(8,128)(2,1)S(1)} %get-tuple-element.6, bf16[4096,128]{1,0:T(8,128)(2,1)S(1)} %get-tuple-element.5), kind=kOutput, calls=%fused_computation.82 | convolution fusion | flops 541097984 | bytes 6488064 | tf_op jit(solution)/shard_map/dot_general | solution.py:50
  119.2 0.1 copy.13
  119.3 0.1 fusion.18
  119.5 5.2 %all_gather.17 = bf16[32,128]{1,0:T(8,128)(2,1)S(1)} all-gather(bf16[8,128]{1,0:T(8,128)(2,1)S(1)} %convert_element_type.28), channel_id=1, replica_groups=mesh['leaf'=8,'sep'=4] {'sep'}, dimensions={0}, use_global_device_ids=true | all-gather | bytes 10240 | tf_op jit(solution)/shard_map/all_gather | solution.py:39
  124.6 0.7 collective-permute-start.8
  125.3 7.2 %all_gather.18 = bf16[2048,128]{1,0:T(8,128)(2,1)S(1)} all-gather(bf16[512,128]{1,0:T(8,128)(2,1)S(1)} %slice.81), channel_id=1, replica_groups=mesh['leaf'=8,'sep'=4] {'sep'}, dimensions={0}, use_global_device_ids=true | all-gather | bytes 655360 | tf_op jit(solution)/shard_map/all_gather | solution.py:39
  132.5 1.1 collective-permute-start.10
  133.6 0.0 collective-permute-done.8
  133.6 0.7 collective-permute-start.9
  134.3 0.0 collective-permute-done.7
  134.3 1.2 broadcast_select_fusion.5
  135.5 1.9 %collective-permute-done.9 = bf16[64,128]{1,0:T(8,128)(2,1)S(1)} collective-permute-done((bf16[64,128]{1,0:T(8,128)(2,1)S(1)}, bf16[64,128]{1,0:T(8,128)(2,1)S(1)}, u32[]{:S(2)}, u32[]{:S(2)}) %collective-permute-start.9) | collective-permute-done | bytes 16416 | tf_op jit(solution)/shard_map/ppermute | solution.py:16
  137.4 0.2 fusion.21
  137.6 0.9 fusion.43
  138.5 0.0 copy-start.5
  138.5 0.1 copy.14
  138.7 0.1 reshape.84
  138.7 0.1 fusion.15
  138.9 5.2 %all_gather.19 = bf16[32,128]{1,0:T(8,128)(2,1)S(1)} all-gather(bf16[8,128]{1,0:T(8,128)(2,1)S(1)} %convert_element_type.30), channel_id=1, replica_groups=mesh['leaf'=8,'sep'=4] {'sep'}, dimensions={0}, use_global_device_ids=true | all-gather | bytes 10240 | tf_op jit(solution)/shard_map/all_gather | solution.py:39
  144.0 0.9 collective-permute-start.11
  144.9 1.8 %collective-permute-done.10 = bf16[2048,128]{1,0:T(8,128)(2,1)} collective-permute-done((bf16[2048,128]{1,0:T(8,128)(2,1)S(1)}, bf16[2048,128]{1,0:T(8,128)(2,1)}, u32[]{:S(2)}, u32[]{:S(2)}) %collective-permute-start.10) | collective-permute-done | bytes 524320 | tf_op jit(solution)/shard_map/ppermute | solution.py:16
  146.8 1.1 broadcast_select_fusion.3
  147.9 0.0 collective-permute-done.11
  147.9 0.2 fusion.25
  148.1 3.8 %fusion.4 = f32[512,128]{0,1:T(8,128)S(1)} fusion(f32[128,512]{1,0:T(8,128)S(1)} %fusion.25, bf16[512,4096]{1,0:T(8,128)(2,1)} %param.11, bf16[2048,128]{1,0:T(8,128)(2,1)S(1)} %get-tuple-element.8, bf16[2048,128]{1,0:T(8,128)(2,1)S(1)} %get-tuple-element.7), kind=kOutput, calls=%fused_computation.5 | convolution fusion | flops 539033600 | bytes 5767168 | tf_op jit(solution)/shard_map/dot_general | solution.py:50
  151.9 0.0 copy-done.6
  152.0 1.0 copy.15
  (33 shorter events, 0.3 us)
Async XLA Ops:
  0.0 137.6 %copy-start = (bf16[256,4096]{1,0:T(8,128)(2,1)S(1)}, bf16[256,4096]{1,0:T(8,128)(2,1)}, u32[]{:S(2)}) copy-start(bf16[256,4096]{1,0:T(8,128)(2,1)} %param.10) | copy-start | bytes 6291460
  1.3 5.6 %collective-permute-start = (f32[32,128]{1,0:T(8,128)S(1)}, f32[32,128]{1,0:T(8,128)S(1)}, u32[]{:S(2)}, u32[]{:S(2)}) collective-permute-start(f32[32,128]{1,0:T(8,128)S(1)} %slice_select_fusion.2), channel_id=1, source_target_pairs={{0,4},{4,0},{8,12},{12,8},{16,20},{20,16},{24,28},{28,24},{1,5},{5... | collective-permute-start | bytes 49160 | tf_op jit(solution)/shard_map/ppermute | solution.py:16
  19.7 4.0 %collective-permute-start.1 = (f32[64,128]{1,0:T(8,128)S(1)}, f32[64,128]{1,0:T(8,128)S(1)}, u32[]{:S(2)}, u32[]{:S(2)}) collective-permute-start(f32[64,128]{1,0:T(8,128)S(1)} %slice_select_fusion), channel_id=1, source_target_pairs={{0,8},{8,0},{4,12},{12,4},{16,24},{24,16},{20,28},{28,20},{1,9},{9... | collective-permute-start | bytes 98312 | tf_op jit(solution)/shard_map/ppermute | solution.py:16
  23.7 3.8 %collective-permute-start.2 = (f32[32,128]{1,0:T(8,128)S(1)}, f32[32,128]{1,0:T(8,128)S(1)}, u32[]{:S(2)}, u32[]{:S(2)}) collective-permute-start(f32[32,128]{1,0:T(8,128)S(1)} %slice_select_fusion.1), channel_id=1, source_target_pairs={{0,4},{4,0},{8,12},{12,8},{16,20},{20,16},{24,28},{28,24},{1,5},{5... | collective-permute-start | bytes 49160 | tf_op jit(solution)/shard_map/ppermute | solution.py:16
  44.5 8.6 %collective-permute-start.3 = (bf16[1024,128]{1,0:T(8,128)(2,1)S(1)}, bf16[1024,128]{1,0:T(8,128)(2,1)S(1)}, u32[]{:S(2)}, u32[]{:S(2)}) collective-permute-start(bf16[1024,128]{1,0:T(8,128)(2,1)S(1)} %all_gather.15), channel_id=1, source_target_pairs={{0,4},{4,0},{8,12},{12,8},{16,20},{20,16},{24,28},{28,24},{1,5},{5... | collective-permute-start | bytes 786440 | tf_op jit(solution)/shard_map/ppermute | solution.py:16
  53.1 13.4 %collective-permute-start.4 = (bf16[2048,128]{1,0:T(8,128)(2,1)S(1)}, bf16[2048,128]{1,0:T(8,128)(2,1)S(1)}, u32[]{:S(2)}, u32[]{:S(2)}) collective-permute-start(bf16[2048,128]{1,0:T(8,128)(2,1)S(1)} %pad_maximum_fusion.1), channel_id=1, source_target_pairs={{0,8},{8,0},{4,12},{12,4},{16,24},{24,16},{20,28},{28,20},{1,9},{9... | collective-permute-start | bytes 1572872 | tf_op jit(solution)/shard_map/ppermute | solution.py:16
  67.8 47.5 %collective-permute-start.5 = (bf16[4096,128]{1,0:T(8,128)(2,1)}, bf16[4096,128]{1,0:T(8,128)(2,1)}, u32[]{:S(2)}, u32[]{:S(2)}) collective-permute-start(bf16[4096,128]{1,0:T(8,128)(2,1)} %pad_maximum_fusion), channel_id=1, source_target_pairs={{0,16},{16,0},{4,20},{20,4},{8,24},{24,8},{12,28},{28,12},{1,17},{... | collective-permute-start | bytes 3145736 | tf_op jit(solution)/shard_map/ppermute | solution.py:16
  76.2 1.6 %copy-start.3 = (bf16[1024,128]{1,0:T(8,128)(2,1)}, bf16[1024,128]{1,0:T(8,128)(2,1)S(1)}, u32[]{:S(2)}) copy-start(bf16[1024,128]{1,0:T(8,128)(2,1)S(1)} %all_gather.16) | copy-start | bytes 786436
  76.2 8.7 %collective-permute-start.6 = (bf16[1024,128]{1,0:T(8,128)(2,1)S(1)}, bf16[1024,128]{1,0:T(8,128)(2,1)}, u32[]{:S(2)}, u32[]{:S(2)}) collective-permute-start(bf16[1024,128]{1,0:T(8,128)(2,1)S(1)} %all_gather.16), channel_id=1, source_target_pairs={{0,4},{4,0},{8,12},{12,8},{16,20},{20,16},{24,28},{28,24},{1,5},{5... | collective-permute-start | bytes 786440 | tf_op jit(solution)/shard_map/ppermute | solution.py:16
  85.9 0.7 copy-start.1
  87.5 29.5 %copy-start.7 = (bf16[256,8192]{1,0:T(8,128)(2,1)S(1)}, bf16[256,8192]{1,0:T(8,128)(2,1)}, u32[]{:S(2)}) copy-start(bf16[256,8192]{1,0:T(8,128)(2,1)} %param.9) | copy-start | bytes 12582916
  87.5 46.8 %collective-permute-start.7 = (bf16[2048,128]{1,0:T(8,128)(2,1)}, bf16[2048,128]{1,0:T(8,128)(2,1)}, u32[]{:S(2)}, u32[]{:S(2)}) collective-permute-start(bf16[2048,128]{1,0:T(8,128)(2,1)} %pad_maximum_fusion.2), channel_id=1, source_target_pairs={{0,8},{8,0},{4,12},{12,4},{16,24},{24,16},{20,28},{28,20},{1,9},{9... | collective-permute-start | bytes 1572872 | tf_op jit(solution)/shard_map/ppermute | solution.py:16
  117.0 17.3 %copy-start.2 = (bf16[1024,128]{1,0:T(8,128)(2,1)S(1)}, bf16[1024,128]{1,0:T(8,128)(2,1)}, u32[]{:S(2)}) copy-start(bf16[1024,128]{1,0:T(8,128)(2,1)} %copy-done.1) | copy-start | bytes 786436
  119.2 18.3 %copy-start.4 = (bf16[256,128]{1,0:T(8,128)(2,1)S(1)}, bf16[256,128]{1,0:T(8,128)(2,1)}, u32[]{:S(2)}) copy-start(bf16[256,128]{1,0:T(8,128)(2,1)} %param.12) | copy-start | bytes 196612
  124.6 9.0 %collective-permute-start.8 = (bf16[32,128]{1,0:T(8,128)(2,1)S(1)}, bf16[32,128]{1,0:T(8,128)(2,1)S(1)}, u32[]{:S(2)}, u32[]{:S(2)}) collective-permute-start(bf16[32,128]{1,0:T(8,128)(2,1)S(1)} %all_gather.17), channel_id=1, source_target_pairs={{0,4},{4,0},{8,12},{12,8},{16,20},{20,16},{24,28},{28,24},{1,5},{5... | collective-permute-start | bytes 24584 | tf_op jit(solution)/shard_map/ppermute | solution.py:16
  132.5 14.3 %collective-permute-start.10 = (bf16[2048,128]{1,0:T(8,128)(2,1)S(1)}, bf16[2048,128]{1,0:T(8,128)(2,1)}, u32[]{:S(2)}, u32[]{:S(2)}) collective-permute-start(bf16[2048,128]{1,0:T(8,128)(2,1)S(1)} %all_gather.18), channel_id=1, source_target_pairs={{0,4},{4,0},{8,12},{12,8},{16,20},{20,16},{24,28},{28,24},{1,5},{5... | collective-permute-start | bytes 1572872 | tf_op jit(solution)/shard_map/ppermute | solution.py:16
  133.6 3.8 %collective-permute-start.9 = (bf16[64,128]{1,0:T(8,128)(2,1)S(1)}, bf16[64,128]{1,0:T(8,128)(2,1)S(1)}, u32[]{:S(2)}, u32[]{:S(2)}) collective-permute-start(bf16[64,128]{1,0:T(8,128)(2,1)S(1)} %pad_maximum_fusion.5), channel_id=1, source_target_pairs={{0,8},{8,0},{4,12},{12,4},{16,24},{24,16},{20,28},{28,20},{1,9},{9... | collective-permute-start | bytes 49160 | tf_op jit(solution)/shard_map/ppermute | solution.py:16
  138.5 9.4 %copy-start.5 = (bf16[512,64]{0,1:T(8,128)(2,1)S(1)}, bf16[512,64]{0,1:T(8,128)(2,1)}, u32[]{:S(2)}) copy-start(bf16[512,64]{0,1:T(8,128)(2,1)} %param.13) | copy-start | bytes 196612
  144.0 3.9 %collective-permute-start.11 = (bf16[32,128]{1,0:T(8,128)(2,1)S(1)}, bf16[32,128]{1,0:T(8,128)(2,1)S(1)}, u32[]{:S(2)}, u32[]{:S(2)}) collective-permute-start(bf16[32,128]{1,0:T(8,128)(2,1)S(1)} %all_gather.19), channel_id=1, source_target_pairs={{0,4},{4,0},{8,12},{12,8},{16,20},{20,16},{24,28},{28,24},{1,5},{5... | collective-permute-start | bytes 24584 | tf_op jit(solution)/shard_map/ppermute | solution.py:16
  148.1 3.8 %copy-start.6 = (f32[256,128]{0,1:T(8,128)S(1)}, f32[256,128]{0,1:T(8,128)}, u32[]{:S(2)}) copy-start(f32[256,128]{0,1:T(8,128)} %get-tuple-element.24) | copy-start | bytes 393220
where the time goes:
time: 154 us; the launch traced here: 153 us
  waiting for transfers between devices  61.5 us (40%)
  blocking collectives  49.8 us (32%)
  starting transfers between devices  15.8 us (10%)
  matrix products  9.76 us (6%)
  other arithmetic  9.43 us (6%)
  local copies, waits for them, and re-layouts  4.34 us (3%)
  between operations  2.28 us (1%)
    ppermute x12, waiting for transfers between devices, from_partner(): return lax.ppermute(block, axis, route)  61.5 us
    all_gather x5, blocking collectives, collect(): panel = lax.all_gather(piece, 'sep', axis=0, tiled=True)  29.1 us
    unnamed x2, blocking collectives  20.8 us
    ppermute x12, starting transfers between devices, from_partner(): return lax.ppermute(block, axis, route)  15.8 us
    dot_general x3, matrix products, apply_inverse(): return jnp.dot(inverse, panel, preferred_element_type=jnp.float32)  6.77 us
    select_n x9, other arithmetic, collect(): first = jnp.where(upper, partner, panel)  5.36 us
  transfers between devices with their start and end apart: 12, of which 8 were waited for; matrix products, arithmetic and copies ran while one was open for 8% of the time, Pallas kernels for 0%

commit v1 on v0

--- a/solution.py
+++ b/solution.py
@@ -4,6 +4,25 @@
 from jax.sharding import PartitionSpec as P
 
 BLOCK = 8
+
+
+def ring_gather(shard, axis, dim):
+    size, place, span = (lax.axis_size(axis), lax.axis_index(axis), shard.shape[dim])
+    right = [(i, (i + 1) % size) for i in range(size)]
+    backward = [(i, (i - 1) % size) for i in range(size)]
+    out = jnp.zeros((*shard.shape[:dim], size * span, *shard.shape[dim + 1 :]), shard.dtype)
+    out = lax.dynamic_update_slice_in_dim(out, shard, place * span, axis=dim)
+    from_left = from_right = shard
+    half = size // 2
+    for lap in range(1, half + 1):
+        from_left = lax.ppermute(from_left, axis, right)
+        out = lax.dynamic_update_slice_in_dim(out, from_left, (place - lap) % size * span, axis=dim)
+        if lap < size - half:
+            from_right = lax.ppermute(from_right, axis, backward)
+            out = lax.dynamic_update_slice_in_dim(
+                out, from_right, (place + lap) % size * span, axis=dim
+            )
+    return out
 
 
 def from_partner(block, axis, distance):
@@ -36,7 +55,7 @@
     lower_side = right_side[2 * dev_rows :]
 
     def collect(piece, depth_bits):
-        panel = lax.all_gather(piece, "sep", axis=0, tiled=True)
+        panel = ring_gather(piece, "sep", 0)
         for bit_index in range(depth_bits):
             partner = from_partner(panel, "leaf", bit_index)
             upper = leaf_index >> bit_index & 1 == 1

time: 154 us -> 147 us (0.955)
  blocking collectives: 49.8 us -> 20.8 us
  waiting for transfers between devices: 61.5 us -> 75.6 us
  starting transfers between devices: 15.8 us -> 23.4 us
  local copies, waits for them, and re-layouts: 4.34 us -> 10.2 us
  other arithmetic: 9.43 us -> 6.52 us
  matrix products: 9.76 us -> 7.93 us
    all_gather x5 -> x0, blocking collectives: 29.1 us -> none  [collect(): panel = lax.all_gather(piece, 'sep', axis=0, tiled=True)]
    ppermute x0 -> x15, waiting for transfers between devices: none -> 20.9 us  [the longest x10 18.1 us: ring_gather(): from_left = lax.ppermute(from_left, axis, right)]
    ppermute x0 -> x15, starting transfers between devices: none -> 7.31 us  [the longest x5 5.64 us: ring_gather(): from_right = lax.ppermute(from_right, axis, backward)]
    ppermute x12, waiting for transfers between devices: 61.5 us -> 54.7 us  [from_partner(): return lax.ppermute(block, axis, route)]
    dynamic_update_slice x0 -> x16, local copies, waits for them, and re-layouts: none -> 6.56 us  [the longest x10 3.21 us: ring_gather(): lax.dynamic_update_slice_in_dim(out, from_left, (place - lap) % size * sp...]
    convert_element_type x4 -> x0, other arithmetic: 1.86 us -> none  [the longest x1 0.92 us: on_device(): middle_words = (middle_side - lower_accum[dev_rows:]).astype(jnp.bfloat16)]
  transfers between devices with their start and end apart: 12 -> 27, of which waited for: 8 -> 18; matrix products, arithmetic and copies ran while one was open for 8% -> 10% of each run, Pallas kernels for 0% -> 0%
where the time goes in v1:
time: 147 us
  waiting for transfers between devices  75.6 us (51%)
  starting transfers between devices  23.4 us (16%)
  blocking collectives  20.8 us (14%)
  local copies, waits for them, and re-layouts  10.2 us (7%)
  matrix products  7.93 us (5%)
  other arithmetic  6.52 us (4%)
  between operations  2.4 us (2%)
    ppermute x12, waiting for transfers between devices, from_partner(): return lax.ppermute(block, axis, route)  54.7 us
    unnamed x2, blocking collectives  20.8 us
    ppermute x10, waiting for transfers between devices, ring_gather(): from_left = lax.ppermute(from_left, axis, right)  18.1 us
    ppermute x12, starting transfers between devices, from_partner(): return lax.ppermute(block, axis, route)  16.1 us
    dot_general x3, matrix products, apply_inverse(): return jnp.dot(inverse, panel, preferred_element_type=jnp.float32)  6.08 us
    ppermute x5, starting transfers between devices, ring_gather(): from_right = lax.ppermute(from_right, axis, backward)  5.64 us
    select_n x9, other arithmetic, collect(): first = jnp.where(upper, partner, panel)  5 us
    dynamic_update_slice x10, local copies, waits for them, and re-layouts, ring_gather(): lax.dynamic_update_slice_in_dim(out, from_left, (place - lap) % size * sp...  3.21 us
  transfers between devices with their start and end apart: 27, of which 18 were waited for; matrix products, arithmetic and copies ran while one was open for 10% of the time, Pallas kernels for 0%

profile of v1, /device:TPU:0, one launch (start us, length us, event | category | flops | bytes accessed | tf_op | source)
XLA Modules:
  0.0 146.9 jit_solution(2363742735692463139)
XLA Ops:
  0.0 0.9 broadcast_in_dim.2
  0.9 1.7 %constant_dynamic-update-slice_fusion.7 = (bf16[2048,128]{1,0:T(8,128)(2,1)}, bf16[512,128]{1,0:T(8,128)(2,1)S(1)}) fusion(bf16[2048,128]{1,0:T(8,128)(2,1)} %broadcast_in_dim.2, s32[]{:T(128)S(6)} %select_n.242, f32[1024,128]{1,0:T(8,128)} %param.8), kind=kLoop, calls=%fused_computation.72 | loop fusion | bytes 393220 | tf_op jit(solution)/shard_map/dynamic_update_slice | solution.py:14
  2.6 1.0 fusion.44
  3.6 3.0 %collective-permute-start = (f32[32,128]{1,0:T(8,128)S(1)}, f32[32,128]{1,0:T(8,128)S(1)}, u32[]{:S(2)}, u32[]{:S(2)}) collective-permute-start(f32[32,128]{1,0:T(8,128)S(1)} %slice_select_fusion.2), channel_id=1, source_target_pairs={{0,4},{4,0},{8,12},{12,8},{16,20},{20,16},{24,28},{28,24},{1,5},{5... | collective-permute-start | bytes 49160 | tf_op jit(solution)/shard_map/ppermute | solution.py:35
  7.3 1.3 dynamic-slice
  9.2 10.7 %all-reduce = f32[32,128]{1,0:T(8,128)S(1)} all-reduce(f32[32,128]{1,0:T(8,128)S(1)} %select_add_fusion.2), channel_id=2, replica_groups=mesh['leaf'=8,'sep'=4] {'sep'}, use_global_device_ids=true, to_apply=%region_0.1.clone | all-reduce | flops 4096 | bytes 32768
  19.9 0.1 broadcast_multiply_fusion
  20.2 0.2 convolution_bitcast_fusion
  20.4 1.6 %collective-permute-start.1 = (f32[64,128]{1,0:T(8,128)S(1)}, f32[64,128]{1,0:T(8,128)S(1)}, u32[]{:S(2)}, u32[]{:S(2)}) collective-permute-start(f32[64,128]{1,0:T(8,128)S(1)} %slice_select_fusion), channel_id=1, source_target_pairs={{0,8},{8,0},{4,12},{12,4},{16,24},{24,16},{20,28},{28,20},{1,9},{9... | collective-permute-start | bytes 98312 | tf_op jit(solution)/shard_map/ppermute | solution.py:35
  22.7 1.7 %collective-permute-done.1 = f32[64,128]{1,0:T(8,128)S(1)} collective-permute-done((f32[64,128]{1,0:T(8,128)S(1)}, f32[64,128]{1,0:T(8,128)S(1)}, u32[]{:S(2)}, u32[]{:S(2)}) %collective-permute-start.1) | collective-permute-done | bytes 32800 | tf_op jit(solution)/shard_map/ppermute | solution.py:35
  24.4 0.6 collective-permute-start.2
  25.0 3.2 %collective-permute-done.2 = f32[32,128]{1,0:T(8,128)S(1)} collective-permute-done((f32[32,128]{1,0:T(8,128)S(1)}, f32[32,128]{1,0:T(8,128)S(1)}, u32[]{:S(2)}, u32[]{:S(2)}) %collective-permute-start.2) | collective-permute-done | bytes 16416 | tf_op jit(solution)/shard_map/ppermute | solution.py:35
  28.2 10.1 %all-reduce.1 = f32[32,128]{1,0:T(8,128)S(1)} all-reduce(f32[32,128]{1,0:T(8,128)S(1)} %select_add_fusion.1), channel_id=3, replica_groups=mesh['leaf'=8,'sep'=4] {'sep'}, use_global_device_ids=true, to_apply=%region_1.2.clone | all-reduce | flops 4096 | bytes 32768
  38.3 0.1 slice_add_fusion
  38.7 1.7 %collective-permute-start.4 = (bf16[256,128]{1,0:T(8,128)(2,1)S(1)}, bf16[256,128]{1,0:T(8,128)(2,1)S(1)}, u32[]{:S(2)}, u32[]{:S(2)}) collective-permute-start(bf16[256,128]{1,0:T(8,128)(2,1)S(1)} %get-tuple-element.14), channel_id=1, source_target_pairs={{0,3},{1,0},{2,1},{3,2},{4,7},{5,4},{6,5},{7,6},{8,11},{9,8},{10,9... | collective-permute-start | bytes 196616 | tf_op jit(solution)/shard_map/ppermute | solution.py:21
  40.3 1.9 %collective-permute-done.3 = bf16[256,128]{1,0:T(8,128)(2,1)S(1)} collective-permute-done((bf16[256,128]{1,0:T(8,128)(2,1)S(1)}, bf16[256,128]{1,0:T(8,128)(2,1)S(1)}, u32[]{:S(2)}, u32[]{:S(2)}) %collective-permute-start.3) | collective-permute-done | bytes 65568 | tf_op jit(solution)/shard_map/ppermute | solution.py:18
  42.3 3.6 %collective-permute-done.5 = bf16[256,128]{1,0:T(8,128)(2,1)S(1)} collective-permute-done((bf16[256,128]{1,0:T(8,128)(2,1)S(1)}, bf16[256,128]{1,0:T(8,128)(2,1)S(1)}, u32[]{:S(2)}, u32[]{:S(2)}) %collective-permute-start.5) | collective-permute-done | bytes 65568 | tf_op jit(solution)/shard_map/ppermute | solution.py:18
  46.0 0.6 collective-permute-start.6
  46.6 6.5 %collective-permute-done.6 = bf16[1024,128]{1,0:T(8,128)(2,1)S(1)} collective-permute-done((bf16[1024,128]{1,0:T(8,128)(2,1)S(1)}, bf16[1024,128]{1,0:T(8,128)(2,1)S(1)}, u32[]{:S(2)}, u32[]{:S(2)}) %collective-permute-start.6) | collective-permute-done | bytes 262176 | tf_op jit(solution)/shard_map/ppermute | solution.py:35
  53.2 1.6 %collective-permute-start.7 = (bf16[2048,128]{1,0:T(8,128)(2,1)S(1)}, bf16[2048,128]{1,0:T(8,128)(2,1)S(1)}, u32[]{:S(2)}, u32[]{:S(2)}) collective-permute-start(bf16[2048,128]{1,0:T(8,128)(2,1)S(1)} %pad_maximum_fusion.1), channel_id=1, source_target_pairs={{0,8},{8,0},{4,12},{12,4},{16,24},{24,16},{20,28},{28,20},{1,9},{9... | collective-permute-start | bytes 1572872 | tf_op jit(solution)/shard_map/ppermute | solution.py:35
  54.8 10.1 %collective-permute-done.7 = bf16[2048,128]{1,0:T(8,128)(2,1)S(1)} collective-permute-done((bf16[2048,128]{1,0:T(8,128)(2,1)S(1)}, bf16[2048,128]{1,0:T(8,128)(2,1)S(1)}, u32[]{:S(2)}, u32[]{:S(2)}) %collective-permute-start.7) | collective-permute-done | bytes 524320 | tf_op jit(solution)/shard_map/ppermute | solution.py:35
  65.0 0.2 broadcast_select_fusion.7
  65.2 1.1 pad_maximum_fusion
  66.3 2.6 %collective-permute-start.8 = (bf16[4096,128]{1,0:T(8,128)(2,1)}, bf16[4096,128]{1,0:T(8,128)(2,1)}, u32[]{:S(2)}, u32[]{:S(2)}) collective-permute-start(bf16[4096,128]{1,0:T(8,128)(2,1)} %pad_maximum_fusion), channel_id=1, source_target_pairs={{0,16},{16,0},{4,20},{20,4},{8,24},{24,8},{12,28},{28,12},{1,17},{... | collective-permute-start | bytes 3145736 | tf_op jit(solution)/shard_map/ppermute | solution.py:35
  68.8 1.0 collective-permute-start.19
  69.8 0.8 collective-permute-start.10
  70.6 1.9 %collective-permute-done.9 = bf16[256,128]{1,0:T(8,128)(2,1)S(1)} collective-permute-done((bf16[256,128]{1,0:T(8,128)(2,1)S(1)}, bf16[256,128]{1,0:T(8,128)(2,1)S(1)}, u32[]{:S(2)}, u32[]{:S(2)}) %collective-permute-start.9) | collective-permute-done | bytes 65568 | tf_op jit(solution)/shard_map/ppermute | solution.py:18
  72.6 0.5 collective-permute-done.10
  73.0 3.2 %collective-permute-done.11 = bf16[256,128]{1,0:T(8,128)(2,1)S(1)} collective-permute-done((bf16[256,128]{1,0:T(8,128)(2,1)S(1)}, bf16[256,128]{1,0:T(8,128)(2,1)S(1)}, u32[]{:S(2)}, u32[]{:S(2)}) %collective-permute-start.11) | collective-permute-done | bytes 65568 | tf_op jit(solution)/shard_map/ppermute | solution.py:18
  76.3 1.8 %collective-permute-start.12 = (bf16[1024,128]{1,0:T(8,128)(2,1)S(1)}, bf16[1024,128]{1,0:T(8,128)(2,1)}, u32[]{:S(2)}, u32[]{:S(2)}) collective-permute-start(bf16[1024,128]{1,0:T(8,128)(2,1)S(1)} %constant_dynamic-update-slice_fusion.12), channel_id=1, source_target_pairs={{0,4},{4,0},{8,12},{12,8},{16,20},{20,16},{24,28},{28,24},{1,5},{5... | collective-permute-start | bytes 786440 | tf_op jit(solution)/shard_map/ppermute | solution.py:35
  78.0 0.5 collective-permute-start.21
  78.5 1.6 %constant_dynamic-update-slice_fusion.6 = bf16[2048,128]{1,0:T(8,128)(2,1)} fusion(bf16[2048,128]{1,0:T(8,128)(2,1)} %get-tuple-element.5, bf16[512,128]{1,0:T(8,128)(2,1)} %collective-permute-done.19, s32[]{:T(128)S(6)} %select_n.243), kind=kLoop, calls=%fused_computation.71 | loop fusion | bytes 262148 | tf_op jit(solution)/shard_map/dynamic_update_slice | solution.py:19
  80.1 1.8 %collective-permute-done.20 = bf16[512,128]{1,0:T(8,128)(2,1)} collective-permute-done((bf16[512,128]{1,0:T(8,128)(2,1)S(1)}, bf16[512,128]{1,0:T(8,128)(2,1)}, u32[]{:S(2)}, u32[]{:S(2)}) %collective-permute-start.20) | collective-permute-done | bytes 131104 | tf_op jit(solution)/shard_map/ppermute | solution.py:21
  81.9 1.6 %constant_dynamic-update-slice_fusion.5 = bf16[2048,128]{1,0:T(8,128)(2,1)} fusion(bf16[2048,128]{1,0:T(8,128)(2,1)} %constant_dynamic-update-slice_fusion.6, bf16[512,128]{1,0:T(8,128)(2,1)} %collective-permute-done.20, s32[]{:T(128)S(6)} %select_n.244), kind=kLoop, calls=%fused_computation.70 | loop fusion | bytes 262148 | tf_op jit(solution)/shard_map/dynamic_update_slice | solution.py:22
  83.4 1.8 %broadcast_select_fusion.9 = (bf16[1024,128]{1,0:T(8,128)(2,1)S(1)}, bf16[1024,128]{1,0:T(8,128)(2,1)}) fusion(bf16[1024,128]{1,0:T(8,128)(2,1)} %collective-permute-done.12, bf16[1024,128]{1,0:T(8,128)(2,1)} %copy-done.2, pred[]{:T(512)S(6)} %eq.112), kind=kLoop, calls=%fused_computation.30 | loop fusion | flops 262144 | bytes 1048577 | tf_op jit(solution)/shard_map/jit(_where)/select_n | solution.py:62
  85.2 26.8 %collective-permute-done.8 = bf16[4096,128]{1,0:T(8,128)(2,1)} collective-permute-done((bf16[4096,128]{1,0:T(8,128)(2,1)}, bf16[4096,128]{1,0:T(8,128)(2,1)}, u32[]{:S(2)}, u32[]{:S(2)}) %collective-permute-start.8) | collective-permute-done | bytes 1048608 | tf_op jit(solution)/shard_map/ppermute | solution.py:35
  112.0 1.6 %broadcast_select_fusion.1 = (bf16[4096,128]{1,0:T(8,128)(2,1)S(1)}, bf16[4096,128]{1,0:T(8,128)(2,1)S(1)}) fusion(bf16[4096,128]{1,0:T(8,128)(2,1)} %collective-permute-done.8, pred[]{:T(512)S(6)} %eq.110, bf16[2048,128]{1,0:T(8,128)(2,1)S(1)} %get-tuple-element.22, bf16[2048,128]{1,0:T(8,128)(2,1)S(1)} %get-tuple-element.21), kind=kLoop, calls=%fused_computation.18 | loop fusion | flops 3145728 | bytes 4194305 | tf_op jit(solution)/shard_map/jit(_where)/select_n | solution.py:62
  113.6 1.5 %fusion.42 = (bf16[256,128]{0,1:T(8,128)(2,1)S(1)}, f32[256,128]{0,1:T(8,128)S(1)}) fusion(bf16[256,8192]{1,0:T(8,128)(2,1)S(1)} %copy-done.9, bf16[4096,128]{1,0:T(8,128)(2,1)S(1)} %get-tuple-element.16, bf16[4096,128]{1,0:T(8,128)(2,1)S(1)} %get-tuple-element.15), kind=kOutput, calls=%fused_computation.102 | convolution fusion | flops 541097984 | bytes 6488064 | tf_op jit(solution)/shard_map/dot_general | solution.py:69
  115.2 0.1 copy.13
  115.3 0.1 fusion.18
  115.6 0.7 collective-permute-start.13
  116.3 1.4 collective-permute-start.15
  117.8 0.8 collective-permute-done.14
  118.5 0.5 collective-permute-done.15
  119.1 2.5 %collective-permute-done.16 = bf16[8,128]{1,0:T(8,128)(2,1)S(1)} collective-permute-done((bf16[8,128]{1,0:T(8,128)(2,1)S(1)}, bf16[8,128]{1,0:T(8,128)(2,1)S(1)}, u32[]{:S(2)}, u32[]{:S(2)}) %collective-permute-start.16) | collective-permute-done | bytes 2080 | tf_op jit(solution)/shard_map/ppermute | solution.py:18
  121.5 2.2 %collective-permute-start.17 = (bf16[32,128]{1,0:T(8,128)(2,1)S(1)}, bf16[32,128]{1,0:T(8,128)(2,1)S(1)}, u32[]{:S(2)}, u32[]{:S(2)}) collective-permute-start(bf16[32,128]{1,0:T(8,128)(2,1)S(1)} %constant_dynamic-update-slice_fusion.8), channel_id=1, source_target_pairs={{0,4},{4,0},{8,12},{12,8},{16,20},{20,16},{24,28},{28,24},{1,5},{5... | collective-permute-start | bytes 24584 | tf_op jit(solution)/shard_map/ppermute | solution.py:35
  123.7 1.6 %constant_dynamic-update-slice_fusion.4 = bf16[2048,128]{1,0:T(8,128)(2,1)} fusion(bf16[2048,128]{1,0:T(8,128)(2,1)} %constant_dynamic-update-slice_fusion.5, bf16[512,128]{1,0:T(8,128)(2,1)} %collective-permute-done.21, s32[]{:T(128)S(6)} %select_n.245), kind=kLoop, calls=%fused_computation.69 | loop fusion | bytes 262148 | tf_op jit(solution)/shard_map/dynamic_update_slice | solution.py:19
  125.4 0.7 collective-permute-start.18
  126.1 4.3 %collective-permute-done.13 = bf16[2048,128]{1,0:T(8,128)(2,1)S(1)} collective-permute-done((bf16[2048,128]{1,0:T(8,128)(2,1)S(1)}, bf16[2048,128]{1,0:T(8,128)(2,1)S(1)}, u32[]{:S(2)}, u32[]{:S(2)}) %collective-permute-start.13) | collective-permute-done | bytes 524320 | tf_op jit(solution)/shard_map/ppermute | solution.py:35
  130.4 0.2 broadcast_select_fusion.5
  130.7 0.2 fusion.21
  130.9 0.9 fusion.43
  131.8 0.1 copy.14
  131.9 0.1 reshape.84
  132.0 0.1 fusion.15
  132.2 1.7 %collective-permute-start.24 = (bf16[8,128]{1,0:T(8,128)(2,1)S(1)}, bf16[8,128]{1,0:T(8,128)(2,1)S(1)}, u32[]{:S(2)}, u32[]{:S(2)}) collective-permute-start(bf16[8,128]{1,0:T(8,128)(2,1)S(1)} %get-tuple-element.8), channel_id=1, source_target_pairs={{0,3},{1,0},{2,1},{3,2},{4,7},{5,4},{6,5},{7,6},{8,11},{9,8},{10,9... | collective-permute-start | bytes 6152 | tf_op jit(solution)/shard_map/ppermute | solution.py:21
  133.9 1.3 collective-permute-done.23
  135.3 3.0 %collective-permute-done.25 = bf16[8,128]{1,0:T(8,128)(2,1)S(1)} collective-permute-done((bf16[8,128]{1,0:T(8,128)(2,1)S(1)}, bf16[8,128]{1,0:T(8,128)(2,1)S(1)}, u32[]{:S(2)}, u32[]{:S(2)}) %collective-permute-start.25) | collective-permute-done | bytes 2080 | tf_op jit(solution)/shard_map/ppermute | solution.py:18
  138.2 0.6 collective-permute-start.26
  138.8 1.1 broadcast_select_fusion.3
  139.9 2.0 %collective-permute-done.26 = bf16[32,128]{1,0:T(8,128)(2,1)S(1)} collective-permute-done((bf16[32,128]{1,0:T(8,128)(2,1)S(1)}, bf16[32,128]{1,0:T(8,128)(2,1)S(1)}, u32[]{:S(2)}, u32[]{:S(2)}) %collective-permute-start.26) | collective-permute-done | bytes 8224 | tf_op jit(solution)/shard_map/ppermute | solution.py:35
  141.9 0.2 fusion.25
  142.1 3.7 %fusion.4 = f32[512,128]{0,1:T(8,128)S(1)} fusion(f32[128,512]{1,0:T(8,128)S(1)} %fusion.25, bf16[512,4096]{1,0:T(8,128)(2,1)} %param.11, bf16[2048,128]{1,0:T(8,128)(2,1)S(1)} %get-tuple-element.18, bf16[2048,128]{1,0:T(8,128)(2,1)S(1)} %get-tuple-element.17), kind=kOutput, calls=%fused_computation.5 | convolution fusion | flops 539033600 | bytes 5767168 | tf_op jit(solution)/shard_map/dot_general | solution.py:69
  145.9 1.0 copy.15
  (82 shorter events, 1.0 us)
Async XLA Ops:
  0.0 130.9 %copy-start = (bf16[256,4096]{1,0:T(8,128)(2,1)S(1)}, bf16[256,4096]{1,0:T(8,128)(2,1)}, u32[]{:S(2)}) copy-start(bf16[256,4096]{1,0:T(8,128)(2,1)} %param.10) | copy-start | bytes 6291460
  0.0 20.1 %copy-start.3 = (f32[1024,128]{1,0:T(8,128)S(1)}, f32[1024,128]{1,0:T(8,128)}, u32[]{:S(2)}) copy-start(f32[1024,128]{1,0:T(8,128)} %param.8) | copy-start | bytes 1572868
  0.0 20.2 %copy-start.4 = (bf16[256,128]{1,0:T(8,128)(2,1)S(1)}, bf16[256,128]{1,0:T(8,128)(2,1)}, u32[]{:S(2)}) copy-start(bf16[256,128]{1,0:T(8,128)(2,1)} %param.12) | copy-start | bytes 196612
  3.6 5.6 %collective-permute-start = (f32[32,128]{1,0:T(8,128)S(1)}, f32[32,128]{1,0:T(8,128)S(1)}, u32[]{:S(2)}, u32[]{:S(2)}) collective-permute-start(f32[32,128]{1,0:T(8,128)S(1)} %slice_select_fusion.2), channel_id=1, source_target_pairs={{0,4},{4,0},{8,12},{12,8},{16,20},{20,16},{24,28},{28,24},{1,5},{5... | collective-permute-start | bytes 49160 | tf_op jit(solution)/shard_map/ppermute | solution.py:35
  20.2 4.2 %copy-start.7 = (bf16[256,128]{1,0:T(8,128)(2,1)}, bf16[256,128]{1,0:T(8,128)(2,1)S(1)}, u32[]{:S(2)}) copy-start(bf16[256,128]{1,0:T(8,128)(2,1)S(1)} %get-tuple-element.10) | copy-start | bytes 196612
  20.4 4.0 %collective-permute-start.1 = (f32[64,128]{1,0:T(8,128)S(1)}, f32[64,128]{1,0:T(8,128)S(1)}, u32[]{:S(2)}, u32[]{:S(2)}) collective-permute-start(f32[64,128]{1,0:T(8,128)S(1)} %slice_select_fusion), channel_id=1, source_target_pairs={{0,8},{8,0},{4,12},{12,4},{16,24},{24,16},{20,28},{28,20},{1,9},{9... | collective-permute-start | bytes 98312 | tf_op jit(solution)/shard_map/ppermute | solution.py:35
  24.4 3.8 %collective-permute-start.2 = (f32[32,128]{1,0:T(8,128)S(1)}, f32[32,128]{1,0:T(8,128)S(1)}, u32[]{:S(2)}, u32[]{:S(2)}) collective-permute-start(f32[32,128]{1,0:T(8,128)S(1)} %slice_select_fusion.1), channel_id=1, source_target_pairs={{0,4},{4,0},{8,12},{12,8},{16,20},{20,16},{24,28},{28,24},{1,5},{5... | collective-permute-start | bytes 49160 | tf_op jit(solution)/shard_map/ppermute | solution.py:35
  38.5 3.7 %collective-permute-start.3 = (bf16[256,128]{1,0:T(8,128)(2,1)S(1)}, bf16[256,128]{1,0:T(8,128)(2,1)S(1)}, u32[]{:S(2)}, u32[]{:S(2)}) collective-permute-start(bf16[256,128]{1,0:T(8,128)(2,1)S(1)} %get-tuple-element.14), channel_id=1, source_target_pairs={{0,1},{1,2},{2,3},{3,0},{4,5},{5,6},{6,7},{7,4},{8,9},{9,10},{10,1... | collective-permute-start | bytes 196616 | tf_op jit(solution)/shard_map/ppermute | solution.py:18
  38.7 3.6 %collective-permute-start.4 = (bf16[256,128]{1,0:T(8,128)(2,1)S(1)}, bf16[256,128]{1,0:T(8,128)(2,1)S(1)}, u32[]{:S(2)}, u32[]{:S(2)}) collective-permute-start(bf16[256,128]{1,0:T(8,128)(2,1)S(1)} %get-tuple-element.14), channel_id=1, source_target_pairs={{0,3},{1,0},{2,1},{3,2},{4,7},{5,4},{6,5},{7,6},{8,11},{9,8},{10,9... | collective-permute-start | bytes 196616 | tf_op jit(solution)/shard_map/ppermute | solution.py:21
  42.3 3.7 %collective-permute-start.5 = (bf16[256,128]{1,0:T(8,128)(2,1)S(1)}, bf16[256,128]{1,0:T(8,128)(2,1)S(1)}, u32[]{:S(2)}, u32[]{:S(2)}) collective-permute-start(bf16[256,128]{1,0:T(8,128)(2,1)S(1)} %collective-permute-done.3), channel_id=1, source_target_pairs={{0,1},{1,2},{2,3},{3,0},{4,5},{5,6},{6,7},{7,4},{8,9},{9,10},{10,1... | collective-permute-start | bytes 196616 | tf_op jit(solution)/shard_map/ppermute | solution.py:18
  46.0 7.1 %collective-permute-start.6 = (bf16[1024,128]{1,0:T(8,128)(2,1)S(1)}, bf16[1024,128]{1,0:T(8,128)(2,1)S(1)}, u32[]{:S(2)}, u32[]{:S(2)}) collective-permute-start(bf16[1024,128]{1,0:T(8,128)(2,1)S(1)} %constant_dynamic-update-slice_fusion.16), channel_id=1, source_target_pairs={{0,4},{4,0},{8,12},{12,8},{16,20},{20,16},{24,28},{28,24},{1,5},{5... | collective-permute-start | bytes 786440 | tf_op jit(solution)/shard_map/ppermute | solution.py:35
  53.2 15.7 %copy-start.8 = (bf16[256,128]{1,0:T(8,128)(2,1)S(1)}, bf16[256,128]{1,0:T(8,128)(2,1)}, u32[]{:S(2)}) copy-start(bf16[256,128]{1,0:T(8,128)(2,1)} %copy-done.7) | copy-start | bytes 196612
  53.2 11.8 %collective-permute-start.7 = (bf16[2048,128]{1,0:T(8,128)(2,1)S(1)}, bf16[2048,128]{1,0:T(8,128)(2,1)S(1)}, u32[]{:S(2)}, u32[]{:S(2)}) collective-permute-start(bf16[2048,128]{1,0:T(8,128)(2,1)S(1)} %pad_maximum_fusion.1), channel_id=1, source_target_pairs={{0,8},{8,0},{4,12},{12,4},{16,24},{24,16},{20,28},{28,20},{1,9},{9... | collective-permute-start | bytes 1572872 | tf_op jit(solution)/shard_map/ppermute | solution.py:35
  66.3 45.7 %collective-permute-start.8 = (bf16[4096,128]{1,0:T(8,128)(2,1)}, bf16[4096,128]{1,0:T(8,128)(2,1)}, u32[]{:S(2)}, u32[]{:S(2)}) collective-permute-start(bf16[4096,128]{1,0:T(8,128)(2,1)} %pad_maximum_fusion), channel_id=1, source_target_pairs={{0,16},{16,0},{4,20},{20,4},{8,24},{24,8},{12,28},{28,12},{1,17},{... | collective-permute-start | bytes 3145736 | tf_op jit(solution)/shard_map/ppermute | solution.py:35
  68.8 3.7 %collective-permute-start.9 = (bf16[256,128]{1,0:T(8,128)(2,1)S(1)}, bf16[256,128]{1,0:T(8,128)(2,1)S(1)}, u32[]{:S(2)}, u32[]{:S(2)}) collective-permute-start(bf16[256,128]{1,0:T(8,128)(2,1)S(1)} %copy-done.8), channel_id=1, source_target_pairs={{0,1},{1,2},{2,3},{3,0},{4,5},{5,6},{6,7},{7,4},{8,9},{9,10},{10,1... | collective-permute-start | bytes 196616 | tf_op jit(solution)/shard_map/ppermute | solution.py:18
  68.8 9.2 %collective-permute-start.19 = (bf16[512,128]{1,0:T(8,128)(2,1)S(1)}, bf16[512,128]{1,0:T(8,128)(2,1)}, u32[]{:S(2)}, u32[]{:S(2)}) collective-permute-start(bf16[512,128]{1,0:T(8,128)(2,1)S(1)} %get-tuple-element.6), channel_id=1, source_target_pairs={{0,1},{1,2},{2,3},{3,0},{4,5},{5,6},{6,7},{7,4},{8,9},{9,10},{10,1... | collective-permute-start | bytes 393224 | tf_op jit(solution)/shard_map/ppermute | solution.py:18
  69.8 3.2 %collective-permute-start.10 = (bf16[256,128]{1,0:T(8,128)(2,1)S(1)}, bf16[256,128]{1,0:T(8,128)(2,1)S(1)}, u32[]{:S(2)}, u32[]{:S(2)}) collective-permute-start(bf16[256,128]{1,0:T(8,128)(2,1)S(1)} %copy-done.8), channel_id=1, source_target_pairs={{0,3},{1,0},{2,1},{3,2},{4,7},{5,4},{6,5},{7,6},{8,11},{9,8},{10,9... | collective-permute-start | bytes 196616 | tf_op jit(solution)/shard_map/ppermute | solution.py:21
  72.5 3.7 %collective-permute-start.11 = (bf16[256,128]{1,0:T(8,128)(2,1)S(1)}, bf16[256,128]{1,0:T(8,128)(2,1)S(1)}, u32[]{:S(2)}, u32[]{:S(2)}) collective-permute-start(bf16[256,128]{1,0:T(8,128)(2,1)S(1)} %collective-permute-done.9), channel_id=1, source_target_pairs={{0,1},{1,2},{2,3},{3,0},{4,5},{5,6},{6,7},{7,4},{8,9},{9,10},{10,1... | collective-permute-start | bytes 196616 | tf_op jit(solution)/shard_map/ppermute | solution.py:18
  76.2 7.2 %copy-start.2 = (bf16[1024,128]{1,0:T(8,128)(2,1)}, bf16[1024,128]{1,0:T(8,128)(2,1)S(1)}, u32[]{:S(2)}) copy-start(bf16[1024,128]{1,0:T(8,128)(2,1)S(1)} %constant_dynamic-update-slice_fusion.12) | copy-start | bytes 786436
  76.3 7.2 %collective-permute-start.12 = (bf16[1024,128]{1,0:T(8,128)(2,1)S(1)}, bf16[1024,128]{1,0:T(8,128)(2,1)}, u32[]{:S(2)}, u32[]{:S(2)}) collective-permute-start(bf16[1024,128]{1,0:T(8,128)(2,1)S(1)} %constant_dynamic-update-slice_fusion.12), channel_id=1, source_target_pairs={{0,4},{4,0},{8,12},{12,8},{16,20},{20,16},{24,28},{28,24},{1,5},{5... | collective-permute-start | bytes 786440 | tf_op jit(solution)/shard_map/ppermute | solution.py:35
  78.0 3.9 %collective-permute-start.20 = (bf16[512,128]{1,0:T(8,128)(2,1)S(1)}, bf16[512,128]{1,0:T(8,128)(2,1)}, u32[]{:S(2)}, u32[]{:S(2)}) collective-permute-start(bf16[512,128]{1,0:T(8,128)(2,1)S(1)} %get-tuple-element.6), channel_id=1, source_target_pairs={{0,3},{1,0},{2,1},{3,2},{4,7},{5,4},{6,5},{7,6},{8,11},{9,8},{10,9... | collective-permute-start | bytes 393224 | tf_op jit(solution)/shard_map/ppermute | solution.py:21
  78.0 45.7 %collective-permute-start.21 = (bf16[512,128]{1,0:T(8,128)(2,1)}, bf16[512,128]{1,0:T(8,128)(2,1)}, u32[]{:S(2)}, u32[]{:S(2)}) collective-permute-start(bf16[512,128]{1,0:T(8,128)(2,1)} %collective-permute-done.19), channel_id=1, source_target_pairs={{0,1},{1,2},{2,3},{3,0},{4,5},{5,6},{6,7},{7,4},{8,9},{9,10},{10,1... | collective-permute-start | bytes 393224 | tf_op jit(solution)/shard_map/ppermute | solution.py:18
  85.2 28.4 %copy-start.9 = (bf16[256,8192]{1,0:T(8,128)(2,1)S(1)}, bf16[256,8192]{1,0:T(8,128)(2,1)}, u32[]{:S(2)}) copy-start(bf16[256,8192]{1,0:T(8,128)(2,1)} %param.9) | copy-start | bytes 12582916
  113.6 1.9 %copy-start.1 = (bf16[1024,128]{1,0:T(8,128)(2,1)S(1)}, bf16[1024,128]{1,0:T(8,128)(2,1)}, u32[]{:S(2)}) copy-start(bf16[1024,128]{1,0:T(8,128)(2,1)} %get-tuple-element.24) | copy-start | bytes 786436
  115.1 15.6 %copy-start.5 = (bf16[256,128]{1,0:T(8,128)(2,1)S(1)}, bf16[256,128]{1,0:T(8,128)(2,1)}, u32[]{:S(2)}) copy-start(bf16[256,128]{1,0:T(8,128)(2,1)} %param.12) | copy-start | bytes 196612
  115.5 3.1 %collective-permute-start.14 = (bf16[8,128]{1,0:T(8,128)(2,1)S(1)}, bf16[8,128]{1,0:T(8,128)(2,1)S(1)}, u32[]{:S(2)}, u32[]{:S(2)}) collective-permute-start(bf16[8,128]{1,0:T(8,128)(2,1)S(1)} %get-tuple-element.12), channel_id=1, source_target_pairs={{0,1},{1,2},{2,3},{3,0},{4,5},{5,6},{6,7},{7,4},{8,9},{9,10},{10,1... | collective-permute-start | bytes 6152 | tf_op jit(solution)/shard_map/ppermute | solution.py:18
  115.6 14.9 %collective-permute-start.13 = (bf16[2048,128]{1,0:T(8,128)(2,1)S(1)}, bf16[2048,128]{1,0:T(8,128)(2,1)S(1)}, u32[]{:S(2)}, u32[]{:S(2)}) collective-permute-start(bf16[2048,128]{1,0:T(8,128)(2,1)S(1)} %pad_maximum_fusion.2), channel_id=1, source_target_pairs={{0,8},{8,0},{4,12},{12,4},{16,24},{24,16},{20,28},{28,20},{1,9},{9... | collective-permute-start | bytes 1572872 | tf_op jit(solution)/shard_map/ppermute | solution.py:35
  116.3 2.7 %collective-permute-start.15 = (bf16[8,128]{1,0:T(8,128)(2,1)S(1)}, bf16[8,128]{1,0:T(8,128)(2,1)S(1)}, u32[]{:S(2)}, u32[]{:S(2)}) collective-permute-start(bf16[8,128]{1,0:T(8,128)(2,1)S(1)} %get-tuple-element.12), channel_id=1, source_target_pairs={{0,3},{1,0},{2,1},{3,2},{4,7},{5,4},{6,5},{7,6},{8,11},{9,8},{10,9... | collective-permute-start | bytes 6152 | tf_op jit(solution)/shard_map/ppermute | solution.py:21
  118.5 3.0 %collective-permute-start.16 = (bf16[8,128]{1,0:T(8,128)(2,1)S(1)}, bf16[8,128]{1,0:T(8,128)(2,1)S(1)}, u32[]{:S(2)}, u32[]{:S(2)}) collective-permute-start(bf16[8,128]{1,0:T(8,128)(2,1)S(1)} %collective-permute-done.14), channel_id=1, source_target_pairs={{0,1},{1,2},{2,3},{3,0},{4,5},{5,6},{6,7},{7,4},{8,9},{9,10},{10,1... | collective-permute-start | bytes 6152 | tf_op jit(solution)/shard_map/ppermute | solution.py:18
  121.5 3.8 %collective-permute-start.17 = (bf16[32,128]{1,0:T(8,128)(2,1)S(1)}, bf16[32,128]{1,0:T(8,128)(2,1)S(1)}, u32[]{:S(2)}, u32[]{:S(2)}) collective-permute-start(bf16[32,128]{1,0:T(8,128)(2,1)S(1)} %constant_dynamic-update-slice_fusion.8), channel_id=1, source_target_pairs={{0,4},{4,0},{8,12},{12,8},{16,20},{20,16},{24,28},{28,24},{1,5},{5... | collective-permute-start | bytes 24584 | tf_op jit(solution)/shard_map/ppermute | solution.py:35
  125.3 13.5 %collective-permute-start.22 = (bf16[2048,128]{1,0:T(8,128)(2,1)}, bf16[2048,128]{1,0:T(8,128)(2,1)S(1)}, u32[]{:S(2)}, u32[]{:S(2)}) collective-permute-start(bf16[2048,128]{1,0:T(8,128)(2,1)} %constant_dynamic-update-slice_fusion.4), channel_id=1, source_target_pairs={{0,4},{4,0},{8,12},{12,8},{16,20},{20,16},{24,28},{28,24},{1,5},{5... | collective-permute-start | bytes 1572872 | tf_op jit(solution)/shard_map/ppermute | solution.py:35
  125.4 5.3 %collective-permute-start.18 = (bf16[64,128]{1,0:T(8,128)(2,1)S(1)}, bf16[64,128]{1,0:T(8,128)(2,1)S(1)}, u32[]{:S(2)}, u32[]{:S(2)}) collective-permute-start(bf16[64,128]{1,0:T(8,128)(2,1)S(1)} %pad_maximum_fusion.5), channel_id=1, source_target_pairs={{0,8},{8,0},{4,12},{12,4},{16,24},{24,16},{20,28},{28,20},{1,9},{9... | collective-permute-start | bytes 49160 | tf_op jit(solution)/shard_map/ppermute | solution.py:35
  131.8 10.1 %copy-start.6 = (bf16[512,64]{0,1:T(8,128)(2,1)S(1)}, bf16[512,64]{0,1:T(8,128)(2,1)}, u32[]{:S(2)}) copy-start(bf16[512,64]{0,1:T(8,128)(2,1)} %param.13) | copy-start | bytes 196612
  132.1 3.1 %collective-permute-start.23 = (bf16[8,128]{1,0:T(8,128)(2,1)S(1)}, bf16[8,128]{1,0:T(8,128)(2,1)S(1)}, u32[]{:S(2)}, u32[]{:S(2)}) collective-permute-start(bf16[8,128]{1,0:T(8,128)(2,1)S(1)} %get-tuple-element.8), channel_id=1, source_target_pairs={{0,1},{1,2},{2,3},{3,0},{4,5},{5,6},{6,7},{7,4},{8,9},{9,10},{10,1... | collective-permute-start | bytes 6152 | tf_op jit(solution)/shard_map/ppermute | solution.py:18
  132.2 3.0 %collective-permute-start.24 = (bf16[8,128]{1,0:T(8,128)(2,1)S(1)}, bf16[8,128]{1,0:T(8,128)(2,1)S(1)}, u32[]{:S(2)}, u32[]{:S(2)}) collective-permute-start(bf16[8,128]{1,0:T(8,128)(2,1)S(1)} %get-tuple-element.8), channel_id=1, source_target_pairs={{0,3},{1,0},{2,1},{3,2},{4,7},{5,4},{6,5},{7,6},{8,11},{9,8},{10,9... | collective-permute-start | bytes 6152 | tf_op jit(solution)/shard_map/ppermute | solution.py:21
  135.2 3.0 %collective-permute-start.25 = (bf16[8,128]{1,0:T(8,128)(2,1)S(1)}, bf16[8,128]{1,0:T(8,128)(2,1)S(1)}, u32[]{:S(2)}, u32[]{:S(2)}) collective-permute-start(bf16[8,128]{1,0:T(8,128)(2,1)S(1)} %collective-permute-done.23), channel_id=1, source_target_pairs={{0,1},{1,2},{2,3},{3,0},{4,5},{5,6},{6,7},{7,4},{8,9},{9,10},{10,1... | collective-permute-start | bytes 6152 | tf_op jit(solution)/shard_map/ppermute | solution.py:18
  138.2 3.7 %collective-permute-start.26 = (bf16[32,128]{1,0:T(8,128)(2,1)S(1)}, bf16[32,128]{1,0:T(8,128)(2,1)S(1)}, u32[]{:S(2)}, u32[]{:S(2)}) collective-permute-start(bf16[32,128]{1,0:T(8,128)(2,1)S(1)} %constant_dynamic-update-slice_fusion), channel_id=1, source_target_pairs={{0,4},{4,0},{8,12},{12,8},{16,20},{20,16},{24,28},{28,24},{1,5},{5... | collective-permute-start | bytes 24584 | tf_op jit(solution)/shard_map/ppermute | solution.py:35
